TPU v7x, 32 devices: a whole 2x2x4 slice. The times are simulated.
32 devices in a mesh: maps: 2 (over y), patch: 8 (over z, x), chan: 2 (over core).
Axes of the slice: x: 2, y: 2, z: 4, core: 2. Of those that a mesh axis runs over, the one named last changes fastest.
Arguments:
- features: bfloat16 [128, 2, 6144], P('chan', 'maps', 'patch'), parts along dimension 1, may hold values from -6 to 6
- out_grad: bfloat16 [128, 2, 6144], P('chan', 'maps', 'patch'), parts along dimension 1, may hold values from -6 to 6
- cheb_weights: bfloat16 [5, 128, 128], P(None, 'chan'), may hold values from -0.5 to 0.5
- band_offsets: int32 [6144, 8], P('patch'), may hold values from -128 to 128, as said below
- edge_weight: bfloat16 [6144, 8], P('patch'), may hold values from 0.099609375 to 10
Outputs:
- input_grad: bfloat16 [128, 2, 6144], P('chan', 'maps', 'patch'), parts along dimension 1
- weight_grad: bfloat16 [10, 128, 128], P('maps', 'chan'), parts along dimension 0
There are 2 independent parts, one for each index of `maps`. A program takes and returns all parts, laid end to end along the dimension named above; an argument that names none is the same for every part. Nothing has to cross between parts.
Inputs may be any that keep to these rules, and one draw needn't show every extreme that they name: p + band_offsets[p, s] is a pixel of the map; some offset equals 128 and some equals -128.
All inputs are finite; a program needn't handle non-finite values.
Results may differ from a plain program's by a relative error of at most 0.006.
Values may be sent and summed in bfloat16 or wider, within the bound.
A program may use at most 64 MiB of HBM per device.

v0:
```python
import jax
import jax.numpy as jnp
from jax import lax
from jax.sharding import PartitionSpec as P

ORDERS = 5
SLOTS = 8
HALO = 128


def extended_2(cells, sides, width):
    for axis, dim in sides:
        count = lax.axis_size(axis)
        ends = count - 1
        head = lax.slice_in_dim(cells, 0, width, axis=dim)
        tail = lax.slice_in_dim(cells, cells.shape[dim] - width, cells.shape[dim], axis=dim)
        cells = jnp.concatenate(
            [
                lax.ppermute(tail, axis, [(i, (i + 1) % count) for i in range(ends)]),
                cells,
                lax.ppermute(head, axis, [((i + 1) % count, i) for i in range(ends)]),
            ],
            axis=dim,
        )
    return cells


def from_behind(block, axis, distance):
    devices = range(lax.axis_size(axis))
    route = [(i - distance, i) for i in devices if i - distance in devices]
    return lax.ppermute(block, axis, route)


def build_matrix(index, weights, width):
    columns = jnp.arange(width, dtype=jnp.int32)[None, :]
    matrix = jnp.zeros((index.shape[0], width), jnp.float32)
    for slot in range(SLOTS):
        hit = (index[:, slot][:, None] == columns).astype(jnp.float32)
        matrix = matrix - weights[:, slot][:, None] * hit
    return matrix


def on_device(features, out_grad, cheb_weights, band_offsets, edge_weight):
    count = features.shape[2]
    weights_f = edge_weight.astype(jnp.float32)
    norm_w = weights_f / jnp.sum(weights_f, axis=1, keepdims=True)
    pixels = count * lax.axis_size("patch")
    scale = 1.0 / (features.shape[1] * pixels) ** 0.5
    place = jnp.arange(count, dtype=jnp.int32)
    ext_index = place[:, None] + HALO + band_offsets
    band_matrix = build_matrix(ext_index, norm_w, count + 2 * HALO)
    full_grad = lax.all_gather(out_grad, "chan", axis=0, tiled=True)
    highest = lax.Precision.HIGHEST

    def forward_op(field):
        extended = extended_2(field, (("patch", 2),), HALO).astype(jnp.float32)
        return jnp.einsum(
            "cbj,pj->cbp",
            extended,
            band_matrix,
            precision=highest,
            preferred_element_type=jnp.float32,
        )

    def adjoint_op(field):
        values = field.astype(jnp.float32)
        buffer = jnp.einsum(
            "cbp,pj->cbj",
            values,
            band_matrix,
            precision=highest,
            preferred_element_type=jnp.float32,
        )
        lower = buffer[:, :, :HALO]
        upper = buffer[:, :, count + HALO :]
        from_above = from_behind(lower.astype(jnp.bfloat16), "patch", -1).astype(lower.dtype)
        from_below = from_behind(upper.astype(jnp.bfloat16), "patch", 1).astype(upper.dtype)
        inner = buffer[:, :, HALO : count + HALO]
        inner = inner.at[:, :, :HALO].add(from_below)
        inner = inner.at[:, :, count - HALO :].add(from_above)
        return inner

    terms = [features]
    sums_each = []
    for order in range(ORDERS):
        if order == 1:
            terms.append(forward_op(features).astype(jnp.bfloat16))
        elif order >= 2:
            nxt = 2.0 * forward_op(terms[order - 1]) - terms[order - 2].astype(jnp.float32)
            terms.append(nxt.astype(jnp.bfloat16))
        sums_each.append(
            lax.psum(
                lax.dot_general(
                    terms[order],
                    full_grad,
                    (((1, 2), (1, 2)), ((), ())),
                    preferred_element_type=jnp.float32,
                ),
                "patch",
            )
        )
    weight_total = jnp.stack(sums_each)
    weight_grad = (weight_total * scale).astype(jnp.bfloat16)
    grads = lax.dot_general(
        cheb_weights, full_grad, (((2,), (0,)), ((), ())), preferred_element_type=jnp.float32
    ).astype(jnp.bfloat16)
    back_4 = grads[4]
    back_3 = (grads[3].astype(jnp.float32) + 2.0 * adjoint_op(back_4)).astype(jnp.bfloat16)
    back_2 = (
        grads[2].astype(jnp.float32) + 2.0 * adjoint_op(back_3) - back_4.astype(jnp.float32)
    ).astype(jnp.bfloat16)
    back_1 = (
        grads[1].astype(jnp.float32) + 2.0 * adjoint_op(back_2) - back_3.astype(jnp.float32)
    ).astype(jnp.bfloat16)
    input_grad = (
        grads[0].astype(jnp.float32) + adjoint_op(back_1) - back_2.astype(jnp.float32)
    ).astype(jnp.bfloat16)
    return (input_grad, weight_grad)


def solution(mesh):
    placed = (
        P("chan", "maps", "patch"),
        P("chan", "maps", "patch"),
        P(None, "chan", None),
        P("patch", None),
        P("patch", None),
    )
    return jax.shard_map(
        on_device,
        mesh=mesh,
        in_specs=placed,
        out_specs=(P("chan", "maps", "patch"), P("maps", "chan", None)),
        check_vma=False,
    )
```

profile of v0, /device:TPU:0, one launch (start us, length us, event | category | flops | bytes accessed | tf_op | source)
XLA Modules:
  0.0 193.3 jit_solution(11666467063485549016)
XLA Ops:
  7.2 0.0 copy-start
  7.2 0.0 all-reduce.3.cloned.1.call-start
  7.2 0.7 fusion.68
  8.0 4.8 %collective-permute-start.8 = (bf16[64,1,128]{2,0,1:T(8,128)(2,1)S(1)}, bf16[64,1,128]{2,0,1:T(8,128)(2,1)S(1)}, u32[]{:S(2)}, u32[]{:S(2)}) collective-permute-start(bf16[64,1,128]{2,0,1:T(8,128)(2,1)S(1)} %get-tuple-element.133), channel_id=1, source_target_pairs={{0,2},{2,4},{4,6},{6,8},{8,10},{10,12},{12,14},{1,3},{3,5},{5,7},{... | collective-permute-start | bytes 49160 | tf_op jit(solution)/shard_map/ppermute | solution.py:19
  12.8 1.3 collective-permute-start.9
  14.1 0.7 convert_reduce_fusion
  14.8 0.7 broadcast_add_fusion
  15.6 0.1 slice_reduce_fusion.15
  15.7 0.7 convert_divide_fusion
  16.4 0.1 slice_reduce_fusion.14
  16.4 2.2 %all_gather.3 = bf16[128,1,768]{2,0,1:T(8,128)(2,1)S(1)} all-gather(bf16[64,1,768]{2,0,1:T(8,128)(2,1)} %param.22), channel_id=1, replica_groups=mesh['maps'=2,'patch'=8,'chan'=2] {'chan'}, dimensions={0}, use_global_device_ids=true | all-gather | bytes 294912 | tf_op jit(solution)/shard_map/all_gather | solution.py:52
  18.6 0.3 convolution_convert_fusion
  18.9 0.0 copy-start.1
  18.9 4.7 %fusion.69 = (bf16[64,1,1024]{2,0,1:T(8,128)(2,1)S(1)}, f32[64,1,1024]{2,0,1:T(8,128)S(1)}) fusion(f32[768]{0:T(1024)S(1)} %get-tuple-element.107, s32[768]{0:T(1024)S(1)} %get-tuple-element.99, f32[768]{0:T(1024)S(1)} %get-tuple-element.108, s32[768]{0:T(1024)S(1)} %get-tuple-element.100, f32[768]{0:T(1024)S(1)} %get-tuple-element.109, ...), kind=kOutput, calls=%fused_computation.136 | convolution fusion | flops 622919680 | bytes 557056 | tf_op jit(solution)/shard_map/cbp,pj->cbj/dot_general | solution.py:67
  23.6 1.3 collective-permute-start.1
  24.9 5.2 %collective-permute-start = (bf16[64,1,128]{2,0,1:T(8,128)(2,1)S(1)}, bf16[64,1,128]{2,0,1:T(8,128)(2,1)S(1)}, u32[]{:S(2)}, u32[]{:S(2)}) collective-permute-start(bf16[64,1,128]{2,0,1:T(8,128)(2,1)S(1)} %get-tuple-element.126), channel_id=1, source_target_pairs={{0,2},{2,4},{4,6},{6,8},{8,10},{10,12},{12,14},{1,3},{3,5},{5,7},{... | collective-permute-start | bytes 49160 | tf_op jit(solution)/shard_map/ppermute | solution.py:31
  30.1 0.8 convolution_bitcast_fusion.8
  31.0 0.0 collective-permute-done.8
  31.0 0.0 collective-permute-done.9
  31.0 5.6 %convolution_convert_fusion.1 = bf16[64,768]{1,0:T(8,128)(2,1)S(1)} fusion(f32[768]{0:T(1024)S(1)} %get-tuple-element.107, s32[768]{0:T(1024)S(1)} %get-tuple-element.99, f32[768]{0:T(1024)S(1)} %get-tuple-element.108, s32[768]{0:T(1024)S(1)} %get-tuple-element.100, f32[768]{0:T(1024)S(1)} %get-tuple-element.109, s32[768]{0:T(1024)S(1)} %get-tuple-element.101, ...), kind=kOutput, calls=%fused_computation.22 | convolution fusion | flops 622903296 | bytes 278528 | tf_op jit(solution)/shard_map/cbj,pj->cbp/dot_general | solution.py:57
  36.7 4.8 %collective-permute-start.10 = (bf16[64,1,128]{2,0,1:T(8,128)(2,1)S(1)}, bf16[64,1,128]{2,0,1:T(8,128)(2,1)S(1)}, u32[]{:S(2)}, u32[]{:S(2)}) collective-permute-start(bf16[64,1,128]{2,0,1:T(8,128)(2,1)S(1)} %get-tuple-element.131), channel_id=1, source_target_pairs={{0,2},{2,4},{4,6},{6,8},{8,10},{10,12},{12,14},{1,3},{3,5},{5,7},{... | collective-permute-start | bytes 49160 | tf_op jit(solution)/shard_map/ppermute | solution.py:19
  41.5 1.5 collective-permute-start.11
  43.0 0.0 collective-permute-done
  43.0 0.0 collective-permute-done.1
  43.0 4.8 %fusion.70 = (bf16[64,1,1024]{2,0,1:T(8,128)(2,1)S(1)}, f32[64,1,1024]{2,0,1:T(8,128)S(1)}) fusion(f32[768]{0:T(1024)S(1)} %get-tuple-element.107, s32[768]{0:T(1024)S(1)} %get-tuple-element.99, f32[768]{0:T(1024)S(1)} %get-tuple-element.108, s32[768]{0:T(1024)S(1)} %get-tuple-element.100, f32[768]{0:T(1024)S(1)} %get-tuple-element.109, ...), kind=kOutput, calls=%fused_computation.137 | convolution fusion | flops 623116288 | bytes 753664 | tf_op jit(solution)/shard_map/cbp,pj->cbj/dot_general | solution.py:67
  47.8 0.8 convolution_bitcast_fusion.7
  48.6 1.3 collective-permute-start.3
  49.9 5.2 %collective-permute-start.2 = (bf16[64,1,128]{2,0,1:T(8,128)(2,1)S(1)}, bf16[64,1,128]{2,0,1:T(8,128)(2,1)S(1)}, u32[]{:S(2)}, u32[]{:S(2)}) collective-permute-start(bf16[64,1,128]{2,0,1:T(8,128)(2,1)S(1)} %get-tuple-element.124), channel_id=1, source_target_pairs={{0,2},{2,4},{4,6},{6,8},{8,10},{10,12},{12,14},{1,3},{3,5},{5,7},{... | collective-permute-start | bytes 49160 | tf_op jit(solution)/shard_map/ppermute | solution.py:31
  55.1 0.0 collective-permute-done.10
  55.1 0.0 collective-permute-done.11
  55.1 5.6 %fusion.5 = bf16[64,1,768]{2,0,1:T(8,128)(2,1)S(1)} fusion(bf16[64,1,768]{2,0,1:T(8,128)(2,1)S(1)} %copy-done.1, f32[768]{0:T(1024)S(1)} %get-tuple-element.107, s32[768]{0:T(1024)S(1)} %get-tuple-element.99, f32[768]{0:T(1024)S(1)} %get-tuple-element.108, s32[768]{0:T(1024)S(1)} %get-tuple-element.100, f32[768]{0:T(1024)S(1)} %get-tuple-element.109, ...), kind=kOutput, calls=%fused_computation.23 | convolution fusion | flops 623050752 | bytes 376832 | tf_op jit(solution)/shard_map/cbj,pj->cbp/dot_general | solution.py:57
  60.8 4.8 %collective-permute-start.12 = (bf16[64,1,128]{2,0,1:T(8,128)(2,1)S(1)}, bf16[64,1,128]{2,0,1:T(8,128)(2,1)S(1)}, u32[]{:S(2)}, u32[]{:S(2)}) collective-permute-start(bf16[64,1,128]{2,0,1:T(8,128)(2,1)S(1)} %get-tuple-element.129), channel_id=1, source_target_pairs={{0,2},{2,4},{4,6},{6,8},{8,10},{10,12},{12,14},{1,3},{3,5},{5,7},{... | collective-permute-start | bytes 49160 | tf_op jit(solution)/shard_map/ppermute | solution.py:19
  65.6 1.3 collective-permute-start.13
  66.9 0.0 collective-permute-done.2
  66.9 0.0 collective-permute-done.3
  67.0 4.7 %fusion.71 = (bf16[64,1,1024]{2,0,1:T(8,128)(2,1)S(1)}, f32[64,1,1024]{2,0,1:T(8,128)S(1)}) fusion(f32[768]{0:T(1024)S(1)} %get-tuple-element.107, s32[768]{0:T(1024)S(1)} %get-tuple-element.99, f32[768]{0:T(1024)S(1)} %get-tuple-element.108, s32[768]{0:T(1024)S(1)} %get-tuple-element.100, f32[768]{0:T(1024)S(1)} %get-tuple-element.109, ...), kind=kOutput, calls=%fused_computation.138 | convolution fusion | flops 622919680 | bytes 540672 | tf_op jit(solution)/shard_map/cbp,pj->cbj/dot_general | solution.py:67
  71.8 0.8 convolution_bitcast_fusion.6
  72.6 1.3 collective-permute-start.5
  73.8 5.4 %collective-permute-start.4 = (bf16[64,1,128]{2,0,1:T(8,128)(2,1)S(1)}, bf16[64,1,128]{2,0,1:T(8,128)(2,1)S(1)}, u32[]{:S(2)}, u32[]{:S(2)}) collective-permute-start(bf16[64,1,128]{2,0,1:T(8,128)(2,1)S(1)} %get-tuple-element.122), channel_id=1, source_target_pairs={{0,2},{2,4},{4,6},{6,8},{8,10},{10,12},{12,14},{1,3},{3,5},{5,7},{... | collective-permute-start | bytes 49160 | tf_op jit(solution)/shard_map/ppermute | solution.py:31
  79.3 0.0 collective-permute-done.12
  79.3 0.0 collective-permute-done.13
  79.3 5.6 %fusion.6 = bf16[64,768]{1,0:T(8,128)(2,1)S(1)} fusion(bf16[64,768]{1,0:T(8,128)(2,1)S(1)} %convolution_convert_fusion.1, f32[768]{0:T(1024)S(1)} %get-tuple-element.107, s32[768]{0:T(1024)S(1)} %get-tuple-element.99, f32[768]{0:T(1024)S(1)} %get-tuple-element.108, s32[768]{0:T(1024)S(1)} %get-tuple-element.100, f32[768]{0:T(1024)S(1)} %get-tuple-element.109, ...), kind=kOutput, calls=%fused_computation.24 | convolution fusion | flops 623050752 | bytes 376832 | tf_op jit(solution)/shard_map/cbj,pj->cbp/dot_general | solution.py:57
  85.0 4.8 %collective-permute-start.14 = (bf16[64,1,128]{2,0,1:T(8,128)(2,1)S(1)}, bf16[64,1,128]{2,0,1:T(8,128)(2,1)S(1)}, u32[]{:S(2)}, u32[]{:S(2)}) collective-permute-start(bf16[64,1,128]{2,0,1:T(8,128)(2,1)S(1)} %get-tuple-element.127), channel_id=1, source_target_pairs={{0,2},{2,4},{4,6},{6,8},{8,10},{10,12},{12,14},{1,3},{3,5},{5,7},{... | collective-permute-start | bytes 49160 | tf_op jit(solution)/shard_map/ppermute | solution.py:19
  89.8 1.3 collective-permute-start.15
  91.1 0.0 collective-permute-done.4
  91.1 0.0 collective-permute-done.5
  91.1 4.8 %fusion.72 = (bf16[64,1,1024]{2,0,1:T(8,128)(2,1)S(1)}, f32[64,1,1024]{2,0,1:T(8,128)S(1)}) fusion(f32[768]{0:T(1024)S(1)} %get-tuple-element.107, s32[768]{0:T(1024)S(1)} %get-tuple-element.99, f32[768]{0:T(1024)S(1)} %get-tuple-element.108, s32[768]{0:T(1024)S(1)} %get-tuple-element.100, f32[768]{0:T(1024)S(1)} %get-tuple-element.109, ...), kind=kOutput, calls=%fused_computation.139 | convolution fusion | flops 623411200 | bytes 1048576 | tf_op jit(solution)/shard_map/cbp,pj->cbj/dot_general | solution.py:67
  95.9 0.8 convolution_bitcast_fusion.5
  96.7 1.3 collective-permute-start.7
  98.0 5.2 %collective-permute-start.6 = (bf16[64,1,128]{2,0,1:T(8,128)(2,1)S(1)}, bf16[64,1,128]{2,0,1:T(8,128)(2,1)S(1)}, u32[]{:S(2)}, u32[]{:S(2)}) collective-permute-start(bf16[64,1,128]{2,0,1:T(8,128)(2,1)S(1)} %get-tuple-element.120), channel_id=1, source_target_pairs={{0,2},{2,4},{4,6},{6,8},{8,10},{10,12},{12,14},{1,3},{3,5},{5,7},{... | collective-permute-start | bytes 49160 | tf_op jit(solution)/shard_map/ppermute | solution.py:31
  103.2 0.0 collective-permute-done.14
  103.2 0.0 collective-permute-done.15
  103.3 5.6 %fusion.8 = bf16[64,768]{1,0:T(8,128)(2,1)S(1)} fusion(bf16[64,1,768]{2,0,1:T(8,128)(2,1)S(1)} %fusion.5, f32[768]{0:T(1024)S(1)} %get-tuple-element.107, s32[768]{0:T(1024)S(1)} %get-tuple-element.99, f32[768]{0:T(1024)S(1)} %get-tuple-element.108, s32[768]{0:T(1024)S(1)} %get-tuple-element.100, f32[768]{0:T(1024)S(1)} %get-tuple-element.109, ...), kind=kOutput, calls=%fused_computation.26 | convolution fusion | flops 623050752 | bytes 376832 | tf_op jit(solution)/shard_map/cbj,pj->cbp/dot_general | solution.py:57
  108.9 0.8 convolution_bitcast_fusion.4
  109.7 0.0 all-reduce.3.cloned.1.call-update
  109.7 0.0 collective-permute-done.6
  109.8 0.7 fusion.14
  110.5 71.6 %all-reduce.3.cloned.1.call-done = (f32[1,64,128]{2,1,0:T(8,128)}, f32[1,64,128]{2,1,0:T(8,128)}, f32[1,64,128]{2,1,0:T(8,128)}, f32[1,64,128]{2,1,0:T(8,128)}, f32[1,64,128]{2,1,0:T(8,128)}) async-done(((f32[1,64,128]{2,1,0:T(8,128)}, f32[1,64,128]{2,1,0:T(8,128)}, f32[1,64,128]{2,1,0:T(8,128)}, f32[1,64,128]{2,1,0:T(8,128)}, f32[1,64,128]{2,1,0:T(8,128)}), (f32[1,64,128]{2,1,0:T(8,128)}, ...) | async-done | bytes 163856 | tf_op jit(solution)/shard_map/psum | solution.py:92
  182.0 0.8 constant_dynamic-update-slice_fusion.4
  182.8 0.8 constant_dynamic-update-slice_fusion.3
  183.6 0.8 constant_dynamic-update-slice_fusion.2
  184.3 0.8 constant_dynamic-update-slice_fusion.1
  185.1 0.8 constant_dynamic-update-slice_fusion
  185.8 0.7 multiply_convert_fusion
  (28 shorter events, 0.3 us)
Async XLA Ops:
  7.2 11.4 %copy-start = (bf16[5,64,128]{2,1,0:T(8,128)(2,1)S(1)}, bf16[5,64,128]{2,1,0:T(8,128)(2,1)}, u32[]{:S(2)}) copy-start(bf16[5,64,128]{2,1,0:T(8,128)(2,1)} %param.23) | copy-start | bytes 245764
  7.2 174.9 %all-reduce.3.cloned.1.call-start = ((), (), s32[]{:S(2)}) async-start(), calls=%async_computation | async-start | bytes 327680 | tf_op jit(solution)/shard_map/psum | solution.py:92
  8.0 23.0 %collective-permute-start.8 = (bf16[64,1,128]{2,0,1:T(8,128)(2,1)S(1)}, bf16[64,1,128]{2,0,1:T(8,128)(2,1)S(1)}, u32[]{:S(2)}, u32[]{:S(2)}) collective-permute-start(bf16[64,1,128]{2,0,1:T(8,128)(2,1)S(1)} %get-tuple-element.133), channel_id=1, source_target_pairs={{0,2},{2,4},{4,6},{6,8},{8,10},{10,12},{12,14},{1,3},{3,5},{5,7},{... | collective-permute-start | bytes 49160 | tf_op jit(solution)/shard_map/ppermute | solution.py:19
  12.8 18.2 %collective-permute-start.9 = (bf16[64,1,128]{2,0,1:T(8,128)(2,1)S(1)}, bf16[64,1,128]{2,0,1:T(8,128)(2,1)S(1)}, u32[]{:S(2)}, u32[]{:S(2)}) collective-permute-start(bf16[64,1,128]{2,0,1:T(8,128)(2,1)S(1)} %get-tuple-element.134), channel_id=1, source_target_pairs={{2,0},{4,2},{6,4},{8,6},{10,8},{12,10},{14,12},{3,1},{5,3},{7,5},{... | collective-permute-start | bytes 49160 | tf_op jit(solution)/shard_map/ppermute | solution.py:21
  18.9 11.2 %copy-start.1 = (bf16[64,1,768]{2,0,1:T(8,128)(2,1)S(1)}, bf16[64,1,768]{2,0,1:T(8,128)(2,1)}, u32[]{:S(2)}) copy-start(bf16[64,1,768]{2,0,1:T(8,128)(2,1)} %param.21) | copy-start | bytes 294916
  23.6 19.3 %collective-permute-start.1 = (bf16[64,1,128]{2,0,1:T(8,128)(2,1)S(1)}, bf16[64,1,128]{2,0,1:T(8,128)(2,1)S(1)}, u32[]{:S(2)}, u32[]{:S(2)}) collective-permute-start(bf16[64,1,128]{2,0,1:T(8,128)(2,1)S(1)} %get-tuple-element.125), channel_id=1, source_target_pairs={{2,0},{4,2},{6,4},{8,6},{10,8},{12,10},{14,12},{3,1},{5,3},{7,5},{... | collective-permute-start | bytes 49160 | tf_op jit(solution)/shard_map/ppermute | solution.py:31
  24.9 18.0 %collective-permute-start = (bf16[64,1,128]{2,0,1:T(8,128)(2,1)S(1)}, bf16[64,1,128]{2,0,1:T(8,128)(2,1)S(1)}, u32[]{:S(2)}, u32[]{:S(2)}) collective-permute-start(bf16[64,1,128]{2,0,1:T(8,128)(2,1)S(1)} %get-tuple-element.126), channel_id=1, source_target_pairs={{0,2},{2,4},{4,6},{6,8},{8,10},{10,12},{12,14},{1,3},{3,5},{5,7},{... | collective-permute-start | bytes 49160 | tf_op jit(solution)/shard_map/ppermute | solution.py:31
  36.7 18.4 %collective-permute-start.10 = (bf16[64,1,128]{2,0,1:T(8,128)(2,1)S(1)}, bf16[64,1,128]{2,0,1:T(8,128)(2,1)S(1)}, u32[]{:S(2)}, u32[]{:S(2)}) collective-permute-start(bf16[64,1,128]{2,0,1:T(8,128)(2,1)S(1)} %get-tuple-element.131), channel_id=1, source_target_pairs={{0,2},{2,4},{4,6},{6,8},{8,10},{10,12},{12,14},{1,3},{3,5},{5,7},{... | collective-permute-start | bytes 49160 | tf_op jit(solution)/shard_map/ppermute | solution.py:19
  41.5 13.6 %collective-permute-start.11 = (bf16[64,1,128]{2,0,1:T(8,128)(2,1)S(1)}, bf16[64,1,128]{2,0,1:T(8,128)(2,1)S(1)}, u32[]{:S(2)}, u32[]{:S(2)}) collective-permute-start(bf16[64,1,128]{2,0,1:T(8,128)(2,1)S(1)} %get-tuple-element.132), channel_id=1, source_target_pairs={{2,0},{4,2},{6,4},{8,6},{10,8},{12,10},{14,12},{3,1},{5,3},{7,5},{... | collective-permute-start | bytes 49160 | tf_op jit(solution)/shard_map/ppermute | solution.py:21
  48.6 18.3 %collective-permute-start.3 = (bf16[64,1,128]{2,0,1:T(8,128)(2,1)S(1)}, bf16[64,1,128]{2,0,1:T(8,128)(2,1)S(1)}, u32[]{:S(2)}, u32[]{:S(2)}) collective-permute-start(bf16[64,1,128]{2,0,1:T(8,128)(2,1)S(1)} %get-tuple-element.123), channel_id=1, source_target_pairs={{2,0},{4,2},{6,4},{8,6},{10,8},{12,10},{14,12},{3,1},{5,3},{7,5},{... | collective-permute-start | bytes 49160 | tf_op jit(solution)/shard_map/ppermute | solution.py:31
  49.9 17.0 %collective-permute-start.2 = (bf16[64,1,128]{2,0,1:T(8,128)(2,1)S(1)}, bf16[64,1,128]{2,0,1:T(8,128)(2,1)S(1)}, u32[]{:S(2)}, u32[]{:S(2)}) collective-permute-start(bf16[64,1,128]{2,0,1:T(8,128)(2,1)S(1)} %get-tuple-element.124), channel_id=1, source_target_pairs={{0,2},{2,4},{4,6},{6,8},{8,10},{10,12},{12,14},{1,3},{3,5},{5,7},{... | collective-permute-start | bytes 49160 | tf_op jit(solution)/shard_map/ppermute | solution.py:31
  60.8 18.5 %collective-permute-start.12 = (bf16[64,1,128]{2,0,1:T(8,128)(2,1)S(1)}, bf16[64,1,128]{2,0,1:T(8,128)(2,1)S(1)}, u32[]{:S(2)}, u32[]{:S(2)}) collective-permute-start(bf16[64,1,128]{2,0,1:T(8,128)(2,1)S(1)} %get-tuple-element.129), channel_id=1, source_target_pairs={{0,2},{2,4},{4,6},{6,8},{8,10},{10,12},{12,14},{1,3},{3,5},{5,7},{... | collective-permute-start | bytes 49160 | tf_op jit(solution)/shard_map/ppermute | solution.py:19
  65.6 13.7 %collective-permute-start.13 = (bf16[64,1,128]{2,0,1:T(8,128)(2,1)S(1)}, bf16[64,1,128]{2,0,1:T(8,128)(2,1)S(1)}, u32[]{:S(2)}, u32[]{:S(2)}) collective-permute-start(bf16[64,1,128]{2,0,1:T(8,128)(2,1)S(1)} %get-tuple-element.130), channel_id=1, source_target_pairs={{2,0},{4,2},{6,4},{8,6},{10,8},{12,10},{14,12},{3,1},{5,3},{7,5},{... | collective-permute-start | bytes 49160 | tf_op jit(solution)/shard_map/ppermute | solution.py:21
  72.6 18.6 %collective-permute-start.5 = (bf16[64,1,128]{2,0,1:T(8,128)(2,1)S(1)}, bf16[64,1,128]{2,0,1:T(8,128)(2,1)S(1)}, u32[]{:S(2)}, u32[]{:S(2)}) collective-permute-start(bf16[64,1,128]{2,0,1:T(8,128)(2,1)S(1)} %get-tuple-element.121), channel_id=1, source_target_pairs={{2,0},{4,2},{6,4},{8,6},{10,8},{12,10},{14,12},{3,1},{5,3},{7,5},{... | collective-permute-start | bytes 49160 | tf_op jit(solution)/shard_map/ppermute | solution.py:31
  73.8 17.3 %collective-permute-start.4 = (bf16[64,1,128]{2,0,1:T(8,128)(2,1)S(1)}, bf16[64,1,128]{2,0,1:T(8,128)(2,1)S(1)}, u32[]{:S(2)}, u32[]{:S(2)}) collective-permute-start(bf16[64,1,128]{2,0,1:T(8,128)(2,1)S(1)} %get-tuple-element.122), channel_id=1, source_target_pairs={{0,2},{2,4},{4,6},{6,8},{8,10},{10,12},{12,14},{1,3},{3,5},{5,7},{... | collective-permute-start | bytes 49160 | tf_op jit(solution)/shard_map/ppermute | solution.py:31
  85.0 18.3 %collective-permute-start.14 = (bf16[64,1,128]{2,0,1:T(8,128)(2,1)S(1)}, bf16[64,1,128]{2,0,1:T(8,128)(2,1)S(1)}, u32[]{:S(2)}, u32[]{:S(2)}) collective-permute-start(bf16[64,1,128]{2,0,1:T(8,128)(2,1)S(1)} %get-tuple-element.127), channel_id=1, source_target_pairs={{0,2},{2,4},{4,6},{6,8},{8,10},{10,12},{12,14},{1,3},{3,5},{5,7},{... | collective-permute-start | bytes 49160 | tf_op jit(solution)/shard_map/ppermute | solution.py:19
  89.8 13.4 %collective-permute-start.15 = (bf16[64,1,128]{2,0,1:T(8,128)(2,1)S(1)}, bf16[64,1,128]{2,0,1:T(8,128)(2,1)S(1)}, u32[]{:S(2)}, u32[]{:S(2)}) collective-permute-start(bf16[64,1,128]{2,0,1:T(8,128)(2,1)S(1)} %get-tuple-element.128), channel_id=1, source_target_pairs={{2,0},{4,2},{6,4},{8,6},{10,8},{12,10},{14,12},{3,1},{5,3},{7,5},{... | collective-permute-start | bytes 49160 | tf_op jit(solution)/shard_map/ppermute | solution.py:21
  96.7 13.0 %collective-permute-start.7 = (bf16[64,1,128]{2,0,1:T(8,128)(2,1)S(1)}, bf16[64,1,128]{2,0,1:T(8,128)(2,1)S(1)}, u32[]{:S(2)}, u32[]{:S(2)}) collective-permute-start(bf16[64,1,128]{2,0,1:T(8,128)(2,1)S(1)} %get-tuple-element.119), channel_id=1, source_target_pairs={{2,0},{4,2},{6,4},{8,6},{10,8},{12,10},{14,12},{3,1},{5,3},{7,5},{... | collective-permute-start | bytes 49160 | tf_op jit(solution)/shard_map/ppermute | solution.py:31
  98.0 11.7 %collective-permute-start.6 = (bf16[64,1,128]{2,0,1:T(8,128)(2,1)S(1)}, bf16[64,1,128]{2,0,1:T(8,128)(2,1)S(1)}, u32[]{:S(2)}, u32[]{:S(2)}) collective-permute-start(bf16[64,1,128]{2,0,1:T(8,128)(2,1)S(1)} %get-tuple-element.120), channel_id=1, source_target_pairs={{0,2},{2,4},{4,6},{6,8},{8,10},{10,12},{12,14},{1,3},{3,5},{5,7},{... | collective-permute-start | bytes 49160 | tf_op jit(solution)/shard_map/ppermute | solution.py:31
Sparse Core Ops, SparseCore 0:
  109.8 72.1 all-reduce.2
where the time goes:
time: 194 us; the launch traced here: 193 us
  waiting for transfers between devices  71.6 us (37%)
  starting transfers between devices  50.7 us (26%)
  matrix products  45.8 us (24%)
  between operations  14.5 us (7%)
  local copies, waits for them, and re-layouts  4.79 us (2%)
  other arithmetic  3.68 us (2%)
  blocking collectives  2.16 us (1%)
    psum x1, waiting for transfers between devices, on_device(): lax.psum(lax.dot_general(terms[order], full_grad, (((1, 2), (1, 2)), ((),...  71.6 us
    ppermute x8, starting transfers between devices, from_behind(): return lax.ppermute(block, axis, route)  26.1 us
    dot_general x4, matrix products, forward_op(): jnp.einsum('cbj,pj->cbp', extended, band_matrix, precision=highest, prefe...  22.5 us
    ppermute x4, starting transfers between devices, extended_2(): lax.ppermute(tail, axis, [(i, (i + 1) % count) for i in range(ends)])  19.3 us
    dot_general x4, matrix products, adjoint_op(): jnp.einsum('cbp,pj->cbj', values, band_matrix, precision=highest, preferr...  19 us
    ppermute x4, starting transfers between devices, extended_2(): lax.ppermute(head, axis, [((i + 1) % count, i) for i in range(ends)])  5.35 us
    dot_general x5, matrix products, on_device(): lax.dot_general(terms[order], full_grad, (((1, 2), (1, 2)), ((), ())), pr...  4.03 us
  transfers between devices with their start and end apart: 17, of which 1 were waited for; matrix products, arithmetic and copies ran while one was open for 25% of the time, Pallas kernels for 0%

commit v1 on v0

v1 whole, which is shorter than its diff:
```python
import functools

import jax
import jax.numpy as jnp
from jax import lax
from jax.experimental import pallas as pl
from jax.experimental.pallas import tpu as pltpu
from jax.sharding import PartitionSpec as P

ORDERS = 5
SLOTS = 8
HALO = 128
FAR = (ORDERS - 1) * HALO
PAIRS = (ORDERS + 1) // 2
SPLIT = 1
MESH = pl.DeviceIdType.MESH
F32 = jnp.float32
BF16 = jnp.bfloat16


def merged(pack):
    offs = pack[0:SLOTS, :].astype(F32)
    w = pack[SLOTS : 2 * SLOTS, :].astype(F32)
    w = w / jnp.sum(w, axis=0, keepdims=True)
    total = w
    for turn in range(1, SLOTS):
        total = total + jnp.where(jnp.roll(offs, turn, axis=0) == offs, jnp.roll(w, turn, axis=0), 0.0)
    return offs, -total


def kernel(patches, fused, x_ref, g_ref, w_ref, off_ref, ew_ref, *refs):
    if fused:
        out_ref, wg_ref = refs[:2]
    else:
        out_ref, raw_ref = refs[:2]
    (pack, gext, bt, gk, fk, xp, wp, part, pin, halo_send, halo_recv, pair_send, pair_recv) = refs[2:15]
    if fused:
        rs_send, rs_recv, ag_send, ag_recv, rss, rsr, ags, agr = refs[15:]
    count = x_ref.shape[1]
    half = x_ref.shape[0]
    tiles = count // HALO
    edge = FAR // HALO
    blocks = (tiles + 2 * edge - 2) // 2
    maps = lax.axis_index("maps")
    me = lax.axis_index("patch")
    chan = lax.axis_index("chan")
    partner = (maps, me, 1 - chan)
    barrier = pltpu.get_barrier_semaphore()
    has_prev = me > 0
    has_next = me < patches - 1

    def greet(dst):
        pl.semaphore_signal(barrier, inc=1, device_id=dst, device_id_type=MESH)

    if fused:
        for d in range(1, patches):
            to = lax.rem(me + d, patches)
            greet((maps, to, chan))
            greet((maps, to, 1 - chan))
        greet(partner)
    else:
        greet((maps, lax.rem(me + 1, patches), chan))
        greet((maps, lax.rem(me + patches - 1, patches), chan))
        greet(partner)

    own = slice(FAR, FAR + count)
    left, right = slice(0, FAR), slice(FAR + count, FAR + count + FAR)
    packed = jnp.concatenate([off_ref[...].astype(F32), ew_ref[...].astype(F32)], axis=0)
    pack[:, own] = packed.astype(BF16)
    gext[:, own] = g_ref[...]

    def empty(side):
        gext[:, side] = jnp.zeros((half, FAR), BF16)
        pack[:, side] = jnp.ones((2 * SLOTS, FAR), BF16)

    pl.when(jnp.logical_not(has_prev))(functools.partial(empty, left))
    pl.when(jnp.logical_not(has_next))(functools.partial(empty, right))

    pl.semaphore_wait(barrier, 2 * patches - 1 if fused else 3)

    def copy(src, dst, send, recv, dev):
        return pltpu.make_async_remote_copy(
            src_ref=src, dst_ref=dst, send_sem=send, recv_sem=recv, device_id=dev, device_id_type=MESH
        )

    head, tail = pl.ds(FAR, FAR), pl.ds(count, FAR)
    lo, hi = pl.ds(0, FAR), pl.ds(FAR + count, FAR)
    prev_dev = (maps, lax.rem(me + patches - 1, patches), chan)
    next_dev = (maps, lax.rem(me + 1, patches), chan)
    to_prev = [
        copy(pack.at[:, head], pack.at[:, hi], halo_send.at[0], halo_recv.at[0], prev_dev),
        copy(gext.at[:, head], gext.at[:, hi], halo_send.at[1], halo_recv.at[1], prev_dev),
    ]
    to_next = [
        copy(pack.at[:, tail], pack.at[:, lo], halo_send.at[2], halo_recv.at[2], next_dev),
        copy(gext.at[:, tail], gext.at[:, lo], halo_send.at[3], halo_recv.at[3], next_dev),
    ]

    def each(copies, name):
        def run():
            for c in copies:
                getattr(c, name)()

        return run

    pl.when(has_next)(each(to_next, "start"))
    pl.when(has_prev)(each(to_prev, "start"))
    to_partner = [
        copy(x_ref, xp, pair_send.at[0], pair_recv.at[0], partner),
        copy(w_ref, wp, pair_send.at[1], pair_recv.at[1], partner),
    ]
    each(to_partner, "start")()

    step = (
        lax.broadcasted_iota(jnp.int32, (HALO, HALO), 0) - lax.broadcasted_iota(jnp.int32, (HALO, HALO), 1)
    ).astype(F32)

    def build(first, last, offs, w):
        for b in range(blocks):
            for u in range(2):
                for v in range(u, u + 3):
                    pt = 2 * b + v
                    if not first <= pt < last:
                        continue
                    cols = slice((pt - first) * HALO, (pt - first + 1) * HALO)
                    o = offs[:, cols] - float(HALO * (u + 1 - v))
                    ws = w[:, cols]
                    tile = jnp.zeros((HALO, HALO), F32)
                    for s in range(SLOTS):
                        tile = jnp.where(o[s : s + 1, :] == step, ws[s : s + 1, :], tile)
                    rows = slice(u * HALO, (u + 1) * HALO)
                    top = tile.astype(BF16)
                    bt[0, b, rows, v * HALO : (v + 1) * HALO] = top
                    if SPLIT == 2:
                        bt[1, b, rows, v * HALO : (v + 1) * HALO] = (tile - top.astype(F32)).astype(BF16)

    def turn_field(first, last):
        for t in range(first, last):
            field = gext[:, t * HALO : (t + 1) * HALO].astype(F32).T
            fk[0, t * HALO : (t + 1) * HALO, :] = field
            gk[0, t * HALO : (t + 1) * HALO, :] = field.astype(BF16)

    def apply(order, b, u0, u1):
        rows = slice(u0 * HALO, u1 * HALO)
        cols = slice(u0 * HALO, (u1 + 2) * HALO)
        base = 2 * b * HALO
        field = gk[order - 1, base + cols.start : base + cols.stop, :]
        total = jnp.dot(bt[0, b, rows, cols], field, preferred_element_type=F32)
        if SPLIT == 2:
            total = total + jnp.dot(bt[1, b, rows, cols], field, preferred_element_type=F32)
        to = slice(base + HALO + rows.start, base + HALO + rows.stop)
        if order >= 2:
            total = 2.0 * total - fk[order - 2, to, :]
        fk[order, to, :] = total
        gk[order, to, :] = total.astype(BF16)

    def sweep(order, skip=()):
        first, last = order, 2 * edge + tiles - order
        for b in range(blocks):
            u0 = 0 if 2 * b + 1 >= first else 1
            u1 = 2 if 2 * b + 3 <= last else 1
            if 2 * b + 1 + u0 >= first and 2 * b + 1 + u1 <= last and u0 < u1 and b not in skip:
                apply(order, b, u0, u1)

    for b in range(blocks):
        for part_no in range(SPLIT):
            bt[part_no, b, 0:HALO, 3 * HALO : 4 * HALO] = jnp.zeros((HALO, HALO), BF16)
            bt[part_no, b, HALO : 2 * HALO, 0:HALO] = jnp.zeros((HALO, HALO), BF16)
    build(edge, edge + tiles, *merged(pack[:, own]))
    turn_field(edge, edge + tiles)
    inner = [b for b in range(blocks) if 2 * b >= edge and 2 * b + 4 <= edge + tiles]
    for b in inner:
        apply(1, b, 0, 2)

    pl.when(has_next)(each(to_prev, "wait_recv"))
    pl.when(has_prev)(each(to_next, "wait_recv"))
    build(0, edge, *merged(pack[:, left]))
    build(edge + tiles, 2 * edge + tiles, *merged(pack[:, right]))
    turn_field(0, edge)
    turn_field(edge + tiles, 2 * edge + tiles)
    sweep(1, inner)
    for order in range(2, ORDERS):
        sweep(order)
    each(to_partner, "wait_recv")()

    grads = []
    for order in range(ORDERS):
        field = gk[order, own, :]
        grads.append(
            [
                jnp.dot(x_ref[...], field, preferred_element_type=F32),
                jnp.dot(xp[...], field, preferred_element_type=F32),
            ]
        )
    if fused:
        size = 2 * half // patches
        zero = jnp.zeros((half, half), F32)
        for side in range(2):
            for m in range(PAIRS):
                second = grads[2 * m + 1][side] if 2 * m + 1 < ORDERS else zero
                both = jnp.concatenate([grads[2 * m][side], second], axis=1).astype(BF16)
                for j in range(patches // 2):
                    rs_send[side * (patches // 2) + j, m * size : (m + 1) * size, :] = both[
                        j * size : (j + 1) * size, :
                    ]
        scatter = []
        for d in range(1, patches):
            to = lax.rem(me + d, patches)
            scatter.append(copy(rs_send.at[to], rs_recv.at[d], rss.at[d], rsr.at[d], (maps, to, chan)))
            scatter[-1].start()
    else:
        for order in range(ORDERS):
            for side in range(2):
                raw_ref[side, order] = grads[order][side]

    mine = jnp.zeros((half, count), F32)
    theirs = jnp.zeros((half, count), F32)
    nt = (((1,), (1,)), ((), ()))
    for order in range(ORDERS):
        field = gk[order, own, :]
        wm = jnp.where(chan == 0, w_ref[order, :, 0:half], w_ref[order, :, half:])
        wt = jnp.where(chan == 0, wp[order, :, 0:half], wp[order, :, half:])
        theirs = theirs + lax.dot_general(wt, field, nt, preferred_element_type=F32)
        mine = mine + lax.dot_general(wm, field, nt, preferred_element_type=F32)
    part[...] = theirs
    swap = copy(part, pin, pair_send.at[2], pair_recv.at[2], partner)
    swap.start()

    if fused:
        total = rs_send[me].astype(F32)
        for d in range(1, patches):
            scatter[d - 1].wait_recv()
            total = total + rs_recv[d].astype(F32)
        scale = 1.0 / (count * patches) ** 0.5
        ag_send[...] = (total * scale).astype(BF16)
        low = me < patches // 2
        goal = jnp.where(low, chan, 1 - chan)
        gather = []
        for d in range(1, patches):
            to = lax.rem(me + d, patches)
            gather.append(copy(ag_send, ag_recv.at[me], ags.at[d], agr.at[me], (maps, to, goal)))
            gather[-1].start()
        across = copy(ag_send, ag_recv.at[me], ags.at[0], agr.at[me], partner)
        pl.when(jnp.logical_not(low))(across.start)

        @pl.when(low)
        def _():
            ag_recv[me] = ag_send[...]

    swap.wait_recv()
    out_ref[...] = (mine + pin[...]).astype(BF16)

    if fused:
        size = 2 * half // patches
        for j in range(patches):
            arrive = copy(ag_send, ag_recv.at[j], ags.at[0], agr.at[j], partner)
            if j < patches // 2:
                pl.when(me != j)(arrive.wait_recv)
            else:
                arrive.wait_recv()
        mid = patches // 2
        for j in range(mid):
            here, there = ag_recv[j], ag_recv[mid + j]
            for order in range(ORDERS):
                rows = slice(order // 2 * size, (order // 2 + 1) * size)
                lanes = slice(order % 2 * half, (order % 2 + 1) * half)
                a, b = here[rows, lanes], there[rows, lanes]
                wg_ref[order, j * size : (j + 1) * size, :] = jnp.where(
                    chan == 0, jnp.concatenate([a, b], axis=1), jnp.concatenate([b, a], axis=1)
                )
        for c in scatter:
            c.wait_send()
        for c in gather:
            c.wait_send()
        pl.when(jnp.logical_not(low))(across.wait_send)
    pl.when(has_next)(each(to_next, "wait_send"))
    pl.when(has_prev)(each(to_prev, "wait_send"))
    each(to_partner, "wait_send")()
    swap.wait_send()


def on_device(features, out_grad, cheb_weights, band_offsets, edge_weight):
    half, _, count = features.shape
    patches = lax.axis_size("patch")
    pixels = count * patches
    size = 2 * half // patches
    fused = patches % 2 == 0 and size % 16 == 0 and size > 0
    wide = count + 2 * FAR
    blocks = (wide // HALO - 2) // 2
    outs = [jax.ShapeDtypeStruct((half, count), BF16)]
    if fused:
        outs.append(jax.ShapeDtypeStruct((ORDERS, half, 2 * half), BF16))
    else:
        outs.append(jax.ShapeDtypeStruct((2, ORDERS, half, half), F32))
    scratch = [
        pltpu.VMEM((2 * SLOTS, wide), BF16),
        pltpu.VMEM((half, wide), BF16),
        pltpu.VMEM((SPLIT, blocks, 2 * HALO, 4 * HALO), BF16),
        pltpu.VMEM((ORDERS, wide, half), BF16),
        pltpu.VMEM((ORDERS, wide, half), F32),
        pltpu.VMEM((half, count), BF16),
        pltpu.VMEM((ORDERS, half, 2 * half), BF16),
        pltpu.VMEM((half, count), F32),
        pltpu.VMEM((half, count), F32),
        pltpu.SemaphoreType.DMA((4,)),
        pltpu.SemaphoreType.DMA((4,)),
        pltpu.SemaphoreType.DMA((3,)),
        pltpu.SemaphoreType.DMA((3,)),
    ]
    if fused:
        piece = (PAIRS * size, 2 * half)
        scratch += [
            pltpu.VMEM((patches,) + piece, BF16),
            pltpu.VMEM((patches,) + piece, BF16),
            pltpu.VMEM(piece, BF16),
            pltpu.VMEM((patches,) + piece, BF16),
            pltpu.SemaphoreType.DMA((patches,)),
            pltpu.SemaphoreType.DMA((patches,)),
            pltpu.SemaphoreType.DMA((patches,)),
            pltpu.SemaphoreType.DMA((patches,)),
        ]
    vmem = pl.BlockSpec(memory_space=pltpu.VMEM)
    grad, weight = pl.pallas_call(
        functools.partial(kernel, patches, fused),
        out_shape=outs,
        in_specs=[vmem] * 5,
        out_specs=[vmem] * 2,
        scratch_shapes=scratch,
        compiler_params=pltpu.CompilerParams(
            collective_id=0, has_side_effects=True, vmem_limit_bytes=40 * 1024 * 1024
        ),
    )(
        features.reshape(half, count),
        out_grad.reshape(half, count),
        cheb_weights,
        band_offsets.T,
        edge_weight.T,
    )
    if not fused:
        weight = lax.psum(weight, "patch") * (1.0 / pixels**0.5)
        near = weight[0]
        far = lax.ppermute(weight[1], "chan", [(0, 1), (1, 0)])
        first = lax.axis_index("chan") == 0
        weight = jnp.where(
            first, jnp.concatenate([near, far], axis=2), jnp.concatenate([far, near], axis=2)
        ).astype(BF16)
    return grad.reshape(half, 1, count), weight


def solution(mesh):
    placed = (
        P("chan", "maps", "patch"),
        P("chan", "maps", "patch"),
        P(None, "chan", None),
        P("patch", None),
        P("patch", None),
    )
    return jax.shard_map(
        on_device,
        mesh=mesh,
        in_specs=placed,
        out_specs=(P("chan", "maps", "patch"), P("maps", "chan", None)),
        check_vma=False,
    )
```

time: 194 us -> 28.6 us (0.15)
  the two profiles are of different devices: /device:TPU:0 before, /device:TPU:1 now
where the time goes in v1:
time: 28.6 us; the launch traced here: 28.3 us
  Pallas kernels  22.3 us (78%)
  local copies, waits for them, and re-layouts  5.39 us (19%)
  between operations  0.65 us (2%)
    pallas_call x1, Pallas kernels, on_device(): pl.pallas_call(functools.partial(kernel, patches, fused), out_shape=outs,...  22.3 us
    unnamed x12, local copies, waits for them, and re-layouts  5.39 us

profile of v1, /device:TPU:1, one launch (start us, length us, event | category | flops | bytes accessed | tf_op | source)
XLA Modules:
  0.0 28.3 jit_solution(14478209165347269679)
XLA Ops:
  0.6 0.0 copy-start
  0.6 0.9 %copy-done = bf16[64,1,768]{2,0,1:T(8,128)(2,1)S(1)} copy-done((bf16[64,1,768]{2,0,1:T(8,128)(2,1)S(1)}, bf16[64,1,768]{2,0,1:T(8,128)(2,1)}, u32[]{:S(2)}) %copy-start) | copy-done | bytes 98328
  1.5 0.0 copy-start.1
  1.5 0.9 %copy-done.1 = bf16[64,1,768]{2,0,1:T(8,128)(2,1)S(1)} copy-done((bf16[64,1,768]{2,0,1:T(8,128)(2,1)S(1)}, bf16[64,1,768]{2,0,1:T(8,128)(2,1)}, u32[]{:S(2)}) %copy-start.1) | copy-done | bytes 98328
  2.4 0.0 copy-start.2
  2.4 0.9 %copy-done.2 = bf16[5,64,128]{2,1,0:T(8,128)(2,1)S(1)} copy-done((bf16[5,64,128]{2,1,0:T(8,128)(2,1)S(1)}, bf16[5,64,128]{2,1,0:T(8,128)(2,1)}, u32[]{:S(2)}) %copy-start.2) | copy-done | bytes 81944
  3.3 0.0 copy-start.3
  3.3 0.7 %copy-done.3 = s32[768,8]{0,1:T(8,128)S(1)} copy-done((s32[768,8]{0,1:T(8,128)S(1)}, s32[768,8]{0,1:T(8,128)}, u32[]{:S(2)}) %copy-start.3) | copy-done | bytes 24600
  4.0 0.0 copy-start.4
  4.0 0.7 %copy-done.4 = bf16[768,8]{0,1:T(8,128)(2,1)S(1)} copy-done((bf16[768,8]{0,1:T(8,128)(2,1)S(1)}, bf16[768,8]{0,1:T(8,128)(2,1)}, u32[]{:S(2)}) %copy-start.4) | copy-done | bytes 12312
  4.8 22.3 %shard_map.68 = (bf16[64,768]{1,0:T(8,128)(2,1)S(1)}, bf16[5,64,128]{2,1,0:T(8,128)(2,1)S(1)}) custom-call(bf16[64,768]{1,0:T(8,128)(2,1)S(1)} %bitcast.5, bf16[64,768]{1,0:T(8,128)(2,1)S(1)} %bitcast.6, bf16[5,64,128]{2,1,0:T(8,128)(2,1)S(1)} %copy-done.2, s32[8,768]{1,0:T(8,128)S(1)} %bitcast.8, bf16[8,768]{1,0:T(8,128)(2,1)S(1)} %bitcast.9), custom_call_target="tpu_custom_call" | custom-call | tf_op jit(solution)/shard_map/pallas_call | solution.py:323
  27.0 0.6 %copy.9 = bf16[64,1,768]{2,0,1:T(8,128)(2,1)} copy(bf16[64,1,768]{2,0,1:T(8,128)(2,1)S(1)} %bitcast.7) | data formatting | bytes 196608
  27.7 0.6 %copy.10 = bf16[5,64,128]{2,1,0:T(8,128)(2,1)} copy(bf16[5,64,128]{2,1,0:T(8,128)(2,1)S(1)} %get-tuple-element.9) | data formatting | bytes 163840
Async XLA Ops:
  0.6 0.9 %copy-start = (bf16[64,1,768]{2,0,1:T(8,128)(2,1)S(1)}, bf16[64,1,768]{2,0,1:T(8,128)(2,1)}, u32[]{:S(2)}) copy-start(bf16[64,1,768]{2,0,1:T(8,128)(2,1)} %param.5) | copy-start | bytes 294916
  1.5 0.9 %copy-start.1 = (bf16[64,1,768]{2,0,1:T(8,128)(2,1)S(1)}, bf16[64,1,768]{2,0,1:T(8,128)(2,1)}, u32[]{:S(2)}) copy-start(bf16[64,1,768]{2,0,1:T(8,128)(2,1)} %param.6) | copy-start | bytes 294916
  2.4 0.9 %copy-start.2 = (bf16[5,64,128]{2,1,0:T(8,128)(2,1)S(1)}, bf16[5,64,128]{2,1,0:T(8,128)(2,1)}, u32[]{:S(2)}) copy-start(bf16[5,64,128]{2,1,0:T(8,128)(2,1)} %w_ref.1) | copy-start | bytes 245764
  3.3 0.7 %copy-start.3 = (s32[768,8]{0,1:T(8,128)S(1)}, s32[768,8]{0,1:T(8,128)}, u32[]{:S(2)}) copy-start(s32[768,8]{0,1:T(8,128)} %param.8) | copy-start | bytes 73732
  4.0 0.7 %copy-start.4 = (bf16[768,8]{0,1:T(8,128)(2,1)S(1)}, bf16[768,8]{0,1:T(8,128)(2,1)}, u32[]{:S(2)}) copy-start(bf16[768,8]{0,1:T(8,128)(2,1)} %param.9) | copy-start | bytes 36868

commit v2 on v1

--- a/solution.py
+++ b/solution.py
@@ -12,7 +12,6 @@
 HALO = 128
 FAR = (ORDERS - 1) * HALO
 PAIRS = (ORDERS + 1) // 2
-SPLIT = 1
 MESH = pl.DeviceIdType.MESH
 F32 = jnp.float32
 BF16 = jnp.bfloat16
@@ -28,19 +27,34 @@
     return offs, -total
 
 
-def kernel(patches, fused, x_ref, g_ref, w_ref, off_ref, ew_ref, *refs):
+def kernel(patches, fused, x_hbm, g_hbm, w_hbm, off_hbm, ew_hbm, *refs):
     if fused:
         out_ref, wg_ref = refs[:2]
     else:
         out_ref, raw_ref = refs[:2]
-    (pack, gext, bt, gk, fk, xp, wp, part, pin, halo_send, halo_recv, pair_send, pair_recv) = refs[2:15]
-    if fused:
-        rs_send, rs_recv, ag_send, ag_recv, rss, rsr, ags, agr = refs[15:]
-    count = x_ref.shape[1]
-    half = x_ref.shape[0]
+    (x_ref, w_ref, off_ref, ew_ref, pack, gext, bt, gk, fk, xp, wp, part, pin) = refs[2:15]
+    load, halo_send, halo_recv, pair_send, pair_recv = refs[15:20]
+    if fused:
+        rs_send, rs_recv, ag_send, ag_recv, rss, rsr, ags, agr, rounds = refs[20:]
+    half, count = x_hbm.shape
+    own = slice(FAR, FAR + count)
+    loads = [
+        pltpu.make_async_copy(src, dst, load.at[n])
+        for n, (src, dst) in enumerate(
+            [
+                (off_hbm, off_ref),
+                (ew_hbm, ew_ref),
+                (g_hbm, gext.at[:, pl.ds(FAR, count)]),
+                (x_hbm, x_ref),
+                (w_hbm, w_ref),
+            ]
+        )
+    ]
+    for c in loads:
+        c.start()
     tiles = count // HALO
     edge = FAR // HALO
-    blocks = (tiles + 2 * edge - 2) // 2
+    wide_tiles = tiles + 2 * edge
     maps = lax.axis_index("maps")
     me = lax.axis_index("patch")
     chan = lax.axis_index("chan")
@@ -49,25 +63,28 @@
     has_prev = me > 0
     has_next = me < patches - 1
 
-    def greet(dst):
-        pl.semaphore_signal(barrier, inc=1, device_id=dst, device_id_type=MESH)
-
-    if fused:
-        for d in range(1, patches):
-            to = lax.rem(me + d, patches)
-            greet((maps, to, chan))
-            greet((maps, to, 1 - chan))
-        greet(partner)
-    else:
-        greet((maps, lax.rem(me + 1, patches), chan))
-        greet((maps, lax.rem(me + patches - 1, patches), chan))
-        greet(partner)
-
-    own = slice(FAR, FAR + count)
+    def present(d):
+        return jnp.logical_and(me + d >= 0, me + d < patches)
+
+    def greet(sem, steps):
+        for d in steps:
+            pl.when(present(d))(
+                functools.partial(
+                    pl.semaphore_signal, sem, inc=1, device_id=(maps, me + d, chan), device_id_type=MESH
+                )
+            )
+
+    def greeted(sem, steps, more=0):
+        pl.semaphore_wait(sem, sum(present(d).astype(jnp.int32) for d in steps) + more)
+
+    near, far = (1, -1, 2, -2), (4, -4)
+    greet(barrier, near)
+    pl.semaphore_signal(barrier, inc=1, device_id=partner, device_id_type=MESH)
     left, right = slice(0, FAR), slice(FAR + count, FAR + count + FAR)
+    loads[0].wait()
+    loads[1].wait()
     packed = jnp.concatenate([off_ref[...].astype(F32), ew_ref[...].astype(F32)], axis=0)
     pack[:, own] = packed.astype(BF16)
-    gext[:, own] = g_ref[...]
 
     def empty(side):
         gext[:, side] = jnp.zeros((half, FAR), BF16)
@@ -76,7 +93,7 @@
     pl.when(jnp.logical_not(has_prev))(functools.partial(empty, left))
     pl.when(jnp.logical_not(has_next))(functools.partial(empty, right))
 
-    pl.semaphore_wait(barrier, 2 * patches - 1 if fused else 3)
+    greeted(barrier, near, 1)
 
     def copy(src, dst, send, recv, dev):
         return pltpu.make_async_remote_copy(
@@ -85,16 +102,17 @@
 
     head, tail = pl.ds(FAR, FAR), pl.ds(count, FAR)
     lo, hi = pl.ds(0, FAR), pl.ds(FAR + count, FAR)
-    prev_dev = (maps, lax.rem(me + patches - 1, patches), chan)
-    next_dev = (maps, lax.rem(me + 1, patches), chan)
-    to_prev = [
-        copy(pack.at[:, head], pack.at[:, hi], halo_send.at[0], halo_recv.at[0], prev_dev),
-        copy(gext.at[:, head], gext.at[:, hi], halo_send.at[1], halo_recv.at[1], prev_dev),
-    ]
-    to_next = [
-        copy(pack.at[:, tail], pack.at[:, lo], halo_send.at[2], halo_recv.at[2], next_dev),
-        copy(gext.at[:, tail], gext.at[:, lo], halo_send.at[3], halo_recv.at[3], next_dev),
-    ]
+    prev_dev = (maps, me - 1, chan)
+    next_dev = (maps, me + 1, chan)
+    to_prev = [copy(pack.at[:, head], pack.at[:, hi], halo_send.at[0], halo_recv.at[0], prev_dev)]
+    to_next = [copy(pack.at[:, tail], pack.at[:, lo], halo_send.at[1], halo_recv.at[1], next_dev)]
+    for c in range(1, edge + 1):
+        src = g_hbm.at[:, pl.ds((c - 1) * HALO, HALO)]
+        dst = gext.at[:, pl.ds(FAR + count + (c - 1) * HALO, HALO)]
+        to_prev.append(copy(src, dst, halo_send.at[2 * c], halo_recv.at[2 * c], prev_dev))
+        src = g_hbm.at[:, pl.ds(count - c * HALO, HALO)]
+        dst = gext.at[:, pl.ds(FAR - c * HALO, HALO)]
+        to_next.append(copy(src, dst, halo_send.at[2 * c + 1], halo_recv.at[2 * c + 1], next_dev))
 
     def each(copies, name):
         def run():
@@ -105,9 +123,11 @@
 
     pl.when(has_next)(each(to_next, "start"))
     pl.when(has_prev)(each(to_prev, "start"))
+    if fused:
+        greet(rounds.at[0], near)
     to_partner = [
-        copy(x_ref, xp, pair_send.at[0], pair_recv.at[0], partner),
-        copy(w_ref, wp, pair_send.at[1], pair_recv.at[1], partner),
+        copy(x_hbm, xp, pair_send.at[0], pair_recv.at[0], partner),
+        copy(w_hbm, wp, pair_send.at[1], pair_recv.at[1], partner),
     ]
     each(to_partner, "start")()
 
@@ -116,75 +136,43 @@
     ).astype(F32)
 
     def build(first, last, offs, w):
-        for b in range(blocks):
-            for u in range(2):
-                for v in range(u, u + 3):
-                    pt = 2 * b + v
-                    if not first <= pt < last:
-                        continue
-                    cols = slice((pt - first) * HALO, (pt - first + 1) * HALO)
-                    o = offs[:, cols] - float(HALO * (u + 1 - v))
-                    ws = w[:, cols]
-                    tile = jnp.zeros((HALO, HALO), F32)
-                    for s in range(SLOTS):
-                        tile = jnp.where(o[s : s + 1, :] == step, ws[s : s + 1, :], tile)
-                    rows = slice(u * HALO, (u + 1) * HALO)
-                    top = tile.astype(BF16)
-                    bt[0, b, rows, v * HALO : (v + 1) * HALO] = top
-                    if SPLIT == 2:
-                        bt[1, b, rows, v * HALO : (v + 1) * HALO] = (tile - top.astype(F32)).astype(BF16)
-
-    def turn_field(first, last):
-        for t in range(first, last):
-            field = gext[:, t * HALO : (t + 1) * HALO].astype(F32).T
-            fk[0, t * HALO : (t + 1) * HALO, :] = field
-            gk[0, t * HALO : (t + 1) * HALO, :] = field.astype(BF16)
-
-    def apply(order, b, u0, u1):
-        rows = slice(u0 * HALO, u1 * HALO)
-        cols = slice(u0 * HALO, (u1 + 2) * HALO)
-        base = 2 * b * HALO
-        field = gk[order - 1, base + cols.start : base + cols.stop, :]
-        total = jnp.dot(bt[0, b, rows, cols], field, preferred_element_type=F32)
-        if SPLIT == 2:
-            total = total + jnp.dot(bt[1, b, rows, cols], field, preferred_element_type=F32)
-        to = slice(base + HALO + rows.start, base + HALO + rows.stop)
+        for pt in range(first, last):
+            cols = slice((pt - first) * HALO, (pt - first + 1) * HALO)
+            ws = w[:, cols]
+            for qt in range(max(pt - 1, 1), min(pt + 1, wide_tiles - 2) + 1):
+                o = offs[:, cols] - float(HALO * (qt - pt))
+                tile = jnp.zeros((HALO, HALO), F32)
+                for s in range(SLOTS):
+                    tile = jnp.where(o[s : s + 1, :] == step, ws[s : s + 1, :], tile)
+                at = (pt - qt + 1) * HALO
+                bt[qt, :, at : at + HALO] = tile.astype(BF16)
+
+    def turn_field(t):
+        field = gext[:, t * HALO : (t + 1) * HALO].astype(F32).T
+        fk[0, t * HALO : (t + 1) * HALO, :] = field
+        gk[0, t * HALO : (t + 1) * HALO, :] = field.astype(BF16)
+
+    def apply(order, t):
+        field = gk[order - 1, (t - 1) * HALO : (t + 2) * HALO, :]
+        total = jnp.dot(bt[t], field, preferred_element_type=F32)
+        to = slice(t * HALO, (t + 1) * HALO)
         if order >= 2:
             total = 2.0 * total - fk[order - 2, to, :]
         fk[order, to, :] = total
         gk[order, to, :] = total.astype(BF16)
 
-    def sweep(order, skip=()):
-        first, last = order, 2 * edge + tiles - order
-        for b in range(blocks):
-            u0 = 0 if 2 * b + 1 >= first else 1
-            u1 = 2 if 2 * b + 3 <= last else 1
-            if 2 * b + 1 + u0 >= first and 2 * b + 1 + u1 <= last and u0 < u1 and b not in skip:
-                apply(order, b, u0, u1)
-
-    for b in range(blocks):
-        for part_no in range(SPLIT):
-            bt[part_no, b, 0:HALO, 3 * HALO : 4 * HALO] = jnp.zeros((HALO, HALO), BF16)
-            bt[part_no, b, HALO : 2 * HALO, 0:HALO] = jnp.zeros((HALO, HALO), BF16)
-    build(edge, edge + tiles, *merged(pack[:, own]))
-    turn_field(edge, edge + tiles)
-    inner = [b for b in range(blocks) if 2 * b >= edge and 2 * b + 4 <= edge + tiles]
-    for b in inner:
-        apply(1, b, 0, 2)
-
-    pl.when(has_next)(each(to_prev, "wait_recv"))
-    pl.when(has_prev)(each(to_next, "wait_recv"))
-    build(0, edge, *merged(pack[:, left]))
-    build(edge + tiles, 2 * edge + tiles, *merged(pack[:, right]))
-    turn_field(0, edge)
-    turn_field(edge + tiles, 2 * edge + tiles)
-    sweep(1, inner)
-    for order in range(2, ORDERS):
-        sweep(order)
-    each(to_partner, "wait_recv")()
+    done = set()
+
+    def advance(first, last):
+        for order in range(1, ORDERS):
+            for t in range(max(first + order, order), min(last - order, wide_tiles - order)):
+                if (order, t) not in done:
+                    done.add((order, t))
+                    apply(order, t)
 
     grads = []
-    for order in range(ORDERS):
+
+    def products(order):
         field = gk[order, own, :]
         grads.append(
             [
@@ -192,6 +180,38 @@
                 jnp.dot(xp[...], field, preferred_element_type=F32),
             ]
         )
+
+    build(edge, edge + tiles, *merged(pack[:, own]))
+    loads[2].wait()
+    for t in range(edge, edge + tiles):
+        turn_field(t)
+    advance(edge, edge + tiles)
+    if fused:
+        greeted(rounds.at[0], near)
+        greet(rounds.at[1], far)
+
+    pl.when(has_next)(to_prev[0].wait_recv)
+    pl.when(has_prev)(to_next[0].wait_recv)
+    build(0, edge, *merged(pack[:, left]))
+    build(edge + tiles, wide_tiles, *merged(pack[:, right]))
+    if fused:
+        greeted(rounds.at[1], far)
+        pl.semaphore_signal(rounds.at[2], inc=1, device_id=partner, device_id_type=MESH)
+    for c in range(1, edge + 1):
+        pl.when(has_next)(to_prev[c].wait_recv)
+        pl.when(has_prev)(to_next[c].wait_recv)
+        turn_field(edge - c)
+        turn_field(edge + tiles - 1 + c)
+        advance(edge - c, edge + tiles + c)
+        if c == 1:
+            each(to_partner, "wait_recv")()
+            loads[3].wait()
+            loads[4].wait()
+            products(0)
+        products(c)
+    if fused:
+        pl.semaphore_wait(rounds.at[2], 1)
+
     if fused:
         size = 2 * half // patches
         zero = jnp.zeros((half, half), F32)
@@ -286,24 +306,28 @@
     size = 2 * half // patches
     fused = patches % 2 == 0 and size % 16 == 0 and size > 0
     wide = count + 2 * FAR
-    blocks = (wide // HALO - 2) // 2
     outs = [jax.ShapeDtypeStruct((half, count), BF16)]
     if fused:
         outs.append(jax.ShapeDtypeStruct((ORDERS, half, 2 * half), BF16))
     else:
         outs.append(jax.ShapeDtypeStruct((2, ORDERS, half, half), F32))
     scratch = [
+        pltpu.VMEM((half, count), BF16),
+        pltpu.VMEM((ORDERS, half, 2 * half), BF16),
+        pltpu.VMEM((SLOTS, count), jnp.int32),
+        pltpu.VMEM((SLOTS, count), BF16),
         pltpu.VMEM((2 * SLOTS, wide), BF16),
         pltpu.VMEM((half, wide), BF16),
-        pltpu.VMEM((SPLIT, blocks, 2 * HALO, 4 * HALO), BF16),
+        pltpu.VMEM((wide // HALO, HALO, 3 * HALO), BF16),
         pltpu.VMEM((ORDERS, wide, half), BF16),
         pltpu.VMEM((ORDERS, wide, half), F32),
         pltpu.VMEM((half, count), BF16),
         pltpu.VMEM((ORDERS, half, 2 * half), BF16),
         pltpu.VMEM((half, count), F32),
         pltpu.VMEM((half, count), F32),
-        pltpu.SemaphoreType.DMA((4,)),
-        pltpu.SemaphoreType.DMA((4,)),
+        pltpu.SemaphoreType.DMA((5,)),
+        pltpu.SemaphoreType.DMA((2 * ORDERS,)),
+        pltpu.SemaphoreType.DMA((2 * ORDERS,)),
         pltpu.SemaphoreType.DMA((3,)),
         pltpu.SemaphoreType.DMA((3,)),
     ]
@@ -318,16 +342,17 @@
             pltpu.SemaphoreType.DMA((patches,)),
             pltpu.SemaphoreType.DMA((patches,)),
             pltpu.SemaphoreType.DMA((patches,)),
+            pltpu.SemaphoreType.REGULAR((3,)),
         ]
     vmem = pl.BlockSpec(memory_space=pltpu.VMEM)
     grad, weight = pl.pallas_call(
         functools.partial(kernel, patches, fused),
         out_shape=outs,
-        in_specs=[vmem] * 5,
+        in_specs=[pl.BlockSpec(memory_space=pltpu.HBM)] * 5,
         out_specs=[vmem] * 2,
         scratch_shapes=scratch,
         compiler_params=pltpu.CompilerParams(
-            collective_id=0, has_side_effects=True, vmem_limit_bytes=40 * 1024 * 1024
+            collective_id=0, has_side_effects=True, vmem_limit_bytes=63 * 1024 * 1024
         ),
     )(
         features.reshape(half, count),

time: 28.6 us -> 25.5 us (0.89)
  the two profiles are of different devices: /device:TPU:1 before, /device:TPU:0 now
where the time goes in v2:
time: 25.5 us; the launch traced here: 25.3 us
  Pallas kernels  22.4 us (88%)
  local copies, waits for them, and re-layouts  2.21 us (9%)
  between operations  0.65 us (3%)
    pallas_call x1, Pallas kernels, on_device(): pl.pallas_call(functools.partial(kernel, patches, fused), out_shape=outs,...  22.4 us
    unnamed x4, local copies, waits for them, and re-layouts  2.21 us

profile of v2, /device:TPU:0, one launch (start us, length us, event | category | flops | bytes accessed | tf_op | source)
XLA Modules:
  0.0 25.3 jit_solution(5533709912722602484)
XLA Ops:
  0.6 22.4 %shard_map.68 = (bf16[64,768]{1,0:T(8,128)(2,1)}, bf16[5,64,128]{2,1,0:T(8,128)(2,1)}) custom-call(bf16[64,768]{1,0:T(8,128)(2,1)} %bitcast.5, bf16[64,768]{1,0:T(8,128)(2,1)} %bitcast.6, bf16[5,64,128]{2,1,0:T(8,128)(2,1)} %w_hbm.1, s32[8,768]{1,0:T(8,128)} %bitcast.8, bf16[8,768]{1,0:T(8,128)(2,1)} %bitcast.9), custom_call_target="tpu_custom_call" | custom-call | tf_op jit(solution)/shard_map/pallas_call | solution.py:348
  23.1 0.0 copy-start
  23.1 1.6 %copy.9 = bf16[64,1,768]{2,0,1:T(8,128)(2,1)} copy(bf16[64,1,768]{2,0,1:T(8,128)(2,1)} %bitcast.7) | data formatting | bytes 196608
  24.7 0.0 copy-done
  24.7 0.6 %copy.10 = bf16[5,64,128]{2,1,0:T(8,128)(2,1)} copy(bf16[5,64,128]{2,1,0:T(8,128)(2,1)S(1)} %copy-done) | data formatting | bytes 163840
Async XLA Ops:
  23.1 1.6 %copy-start = (bf16[5,64,128]{2,1,0:T(8,128)(2,1)S(1)}, bf16[5,64,128]{2,1,0:T(8,128)(2,1)}, u32[]{:S(2)}) copy-start(bf16[5,64,128]{2,1,0:T(8,128)(2,1)} %get-tuple-element.9) | copy-start | bytes 245764

commit v3 on v2

--- a/solution.py
+++ b/solution.py
@@ -106,13 +106,10 @@
     next_dev = (maps, me + 1, chan)
     to_prev = [copy(pack.at[:, head], pack.at[:, hi], halo_send.at[0], halo_recv.at[0], prev_dev)]
     to_next = [copy(pack.at[:, tail], pack.at[:, lo], halo_send.at[1], halo_recv.at[1], next_dev)]
-    for c in range(1, edge + 1):
-        src = g_hbm.at[:, pl.ds((c - 1) * HALO, HALO)]
-        dst = gext.at[:, pl.ds(FAR + count + (c - 1) * HALO, HALO)]
-        to_prev.append(copy(src, dst, halo_send.at[2 * c], halo_recv.at[2 * c], prev_dev))
-        src = g_hbm.at[:, pl.ds(count - c * HALO, HALO)]
-        dst = gext.at[:, pl.ds(FAR - c * HALO, HALO)]
-        to_next.append(copy(src, dst, halo_send.at[2 * c + 1], halo_recv.at[2 * c + 1], next_dev))
+    src = g_hbm.at[:, pl.ds(0, FAR)]
+    to_prev.append(copy(src, gext.at[:, hi], halo_send.at[2], halo_recv.at[2], prev_dev))
+    src = g_hbm.at[:, pl.ds(count - FAR, FAR)]
+    to_next.append(copy(src, gext.at[:, lo], halo_send.at[3], halo_recv.at[3], next_dev))
 
     def each(copies, name):
         def run():
@@ -131,6 +128,7 @@
     ]
     each(to_partner, "start")()
 
+    nt = (((1,), (1,)), ((), ()))
     step = (
         lax.broadcasted_iota(jnp.int32, (HALO, HALO), 0) - lax.broadcasted_iota(jnp.int32, (HALO, HALO), 1)
     ).astype(F32)
@@ -148,18 +146,18 @@
                 bt[qt, :, at : at + HALO] = tile.astype(BF16)
 
     def turn_field(t):
-        field = gext[:, t * HALO : (t + 1) * HALO].astype(F32).T
-        fk[0, t * HALO : (t + 1) * HALO, :] = field
-        gk[0, t * HALO : (t + 1) * HALO, :] = field.astype(BF16)
+        field = gext[:, t * HALO : (t + 1) * HALO]
+        fk[0, :, t * HALO : (t + 1) * HALO] = field.astype(F32)
+        gk[0, :, t * HALO : (t + 1) * HALO] = field
 
     def apply(order, t):
-        field = gk[order - 1, (t - 1) * HALO : (t + 2) * HALO, :]
-        total = jnp.dot(bt[t], field, preferred_element_type=F32)
+        field = gk[order - 1, :, (t - 1) * HALO : (t + 2) * HALO]
+        total = lax.dot_general(field, bt[t], nt, preferred_element_type=F32)
         to = slice(t * HALO, (t + 1) * HALO)
         if order >= 2:
-            total = 2.0 * total - fk[order - 2, to, :]
-        fk[order, to, :] = total
-        gk[order, to, :] = total.astype(BF16)
+            total = 2.0 * total - fk[order - 2, :, to]
+        fk[order, :, to] = total
+        gk[order, :, to] = total.astype(BF16)
 
     done = set()
 
@@ -173,11 +171,11 @@
     grads = []
 
     def products(order):
-        field = gk[order, own, :]
+        field = gk[order, :, own]
         grads.append(
             [
-                jnp.dot(x_ref[...], field, preferred_element_type=F32),
-                jnp.dot(xp[...], field, preferred_element_type=F32),
+                lax.dot_general(x_ref[...], field, nt, preferred_element_type=F32),
+                lax.dot_general(xp[...], field, nt, preferred_element_type=F32),
             ]
         )
 
@@ -197,18 +195,18 @@
     if fused:
         greeted(rounds.at[1], far)
         pl.semaphore_signal(rounds.at[2], inc=1, device_id=partner, device_id_type=MESH)
-    for c in range(1, edge + 1):
-        pl.when(has_next)(to_prev[c].wait_recv)
-        pl.when(has_prev)(to_next[c].wait_recv)
-        turn_field(edge - c)
-        turn_field(edge + tiles - 1 + c)
-        advance(edge - c, edge + tiles + c)
-        if c == 1:
-            each(to_partner, "wait_recv")()
-            loads[3].wait()
-            loads[4].wait()
-            products(0)
-        products(c)
+    each(to_partner, "wait_recv")()
+    loads[3].wait()
+    loads[4].wait()
+    products(0)
+    pl.when(has_next)(to_prev[1].wait_recv)
+    pl.when(has_prev)(to_next[1].wait_recv)
+    for t in range(edge):
+        turn_field(t)
+        turn_field(edge + tiles + t)
+    advance(0, wide_tiles)
+    for order in range(1, ORDERS):
+        products(order)
     if fused:
         pl.semaphore_wait(rounds.at[2], 1)
 
@@ -235,13 +233,12 @@
 
     mine = jnp.zeros((half, count), F32)
     theirs = jnp.zeros((half, count), F32)
-    nt = (((1,), (1,)), ((), ()))
     for order in range(ORDERS):
-        field = gk[order, own, :]
+        field = gk[order, :, own]
         wm = jnp.where(chan == 0, w_ref[order, :, 0:half], w_ref[order, :, half:])
         wt = jnp.where(chan == 0, wp[order, :, 0:half], wp[order, :, half:])
-        theirs = theirs + lax.dot_general(wt, field, nt, preferred_element_type=F32)
-        mine = mine + lax.dot_general(wm, field, nt, preferred_element_type=F32)
+        theirs = theirs + jnp.dot(wt, field, preferred_element_type=F32)
+        mine = mine + jnp.dot(wm, field, preferred_element_type=F32)
     part[...] = theirs
     swap = copy(part, pin, pair_send.at[2], pair_recv.at[2], partner)
     swap.start()
@@ -319,15 +316,15 @@
         pltpu.VMEM((2 * SLOTS, wide), BF16),
         pltpu.VMEM((half, wide), BF16),
         pltpu.VMEM((wide // HALO, HALO, 3 * HALO), BF16),
-        pltpu.VMEM((ORDERS, wide, half), BF16),
-        pltpu.VMEM((ORDERS, wide, half), F32),
+        pltpu.VMEM((ORDERS, half, wide), BF16),
+        pltpu.VMEM((ORDERS, half, wide), F32),
         pltpu.VMEM((half, count), BF16),
         pltpu.VMEM((ORDERS, half, 2 * half), BF16),
         pltpu.VMEM((half, count), F32),
         pltpu.VMEM((half, count), F32),
         pltpu.SemaphoreType.DMA((5,)),
-        pltpu.SemaphoreType.DMA((2 * ORDERS,)),
-        pltpu.SemaphoreType.DMA((2 * ORDERS,)),
+        pltpu.SemaphoreType.DMA((4,)),
+        pltpu.SemaphoreType.DMA((4,)),
         pltpu.SemaphoreType.DMA((3,)),
         pltpu.SemaphoreType.DMA((3,)),
     ]

time: 25.5 us -> 23 us (0.902)
  Pallas kernels: 22.4 us -> 20 us
    pallas_call x1, Pallas kernels: 22.4 us -> 20 us  [on_device(): pl.pallas_call(functools.partial(kernel, patches, fused), out_shape=outs,...]
where the time goes in v3:
time: 23 us; the launch traced here: 22.8 us
  Pallas kernels  20 us (87%)
  local copies, waits for them, and re-layouts  2.21 us (10%)
  between operations  0.65 us (3%)
    pallas_call x1, Pallas kernels, on_device(): pl.pallas_call(functools.partial(kernel, patches, fused), out_shape=outs,...  20 us
    unnamed x4, local copies, waits for them, and re-layouts  2.21 us

profile of v3, /device:TPU:0, one launch (start us, length us, event | category | flops | bytes accessed | tf_op | source)
XLA Modules:
  0.0 22.8 jit_solution(17715687509633650776)
XLA Ops:
  0.6 20.0 %shard_map.68 = (bf16[64,768]{1,0:T(8,128)(2,1)}, bf16[5,64,128]{2,1,0:T(8,128)(2,1)}) custom-call(bf16[64,768]{1,0:T(8,128)(2,1)} %bitcast.5, bf16[64,768]{1,0:T(8,128)(2,1)} %bitcast.6, bf16[5,64,128]{2,1,0:T(8,128)(2,1)} %w_hbm.1, s32[8,768]{1,0:T(8,128)} %bitcast.8, bf16[8,768]{1,0:T(8,128)(2,1)} %bitcast.9), custom_call_target="tpu_custom_call" | custom-call | tf_op jit(solution)/shard_map/pallas_call | solution.py:345
  20.6 0.0 copy-start
  20.6 1.6 %copy.9 = bf16[64,1,768]{2,0,1:T(8,128)(2,1)} copy(bf16[64,1,768]{2,0,1:T(8,128)(2,1)} %bitcast.7) | data formatting | bytes 196608
  22.2 0.0 copy-done
  22.2 0.6 %copy.10 = bf16[5,64,128]{2,1,0:T(8,128)(2,1)} copy(bf16[5,64,128]{2,1,0:T(8,128)(2,1)S(1)} %copy-done) | data formatting | bytes 163840
Async XLA Ops:
  20.6 1.6 %copy-start = (bf16[5,64,128]{2,1,0:T(8,128)(2,1)S(1)}, bf16[5,64,128]{2,1,0:T(8,128)(2,1)}, u32[]{:S(2)}) copy-start(bf16[5,64,128]{2,1,0:T(8,128)(2,1)} %get-tuple-element.9) | copy-start | bytes 245764

commit v4 on v3

--- a/solution.py
+++ b/solution.py
@@ -29,13 +29,13 @@
 
 def kernel(patches, fused, x_hbm, g_hbm, w_hbm, off_hbm, ew_hbm, *refs):
     if fused:
-        out_ref, wg_ref = refs[:2]
+        out_hbm, wg_hbm = refs[:2]
     else:
-        out_ref, raw_ref = refs[:2]
-    (x_ref, w_ref, off_ref, ew_ref, pack, gext, bt, gk, fk, xp, wp, part, pin) = refs[2:15]
-    load, halo_send, halo_recv, pair_send, pair_recv = refs[15:20]
-    if fused:
-        rs_send, rs_recv, ag_send, ag_recv, rss, rsr, ags, agr, rounds = refs[20:]
+        out_hbm, wg_hbm = refs[:2]
+    (out_ref, wg_ref, store, x_ref, w_ref, off_ref, ew_ref, pack, gext, bt, gk, fk, xp, wp, part, pin) = refs[2:18]
+    load, halo_send, halo_recv, pair_send, pair_recv = refs[18:23]
+    if fused:
+        rs_send, rs_recv, ag_send, ag_recv, rss, rsr, ags, agr, rounds = refs[23:]
     half, count = x_hbm.shape
     own = slice(FAR, FAR + count)
     loads = [
@@ -221,15 +221,16 @@
                     rs_send[side * (patches // 2) + j, m * size : (m + 1) * size, :] = both[
                         j * size : (j + 1) * size, :
                     ]
+        order_of = sorted(range(1, patches), key=lambda d: -min(d, patches - d))
         scatter = []
-        for d in range(1, patches):
+        for d in order_of:
             to = lax.rem(me + d, patches)
             scatter.append(copy(rs_send.at[to], rs_recv.at[d], rss.at[d], rsr.at[d], (maps, to, chan)))
             scatter[-1].start()
     else:
         for order in range(ORDERS):
             for side in range(2):
-                raw_ref[side, order] = grads[order][side]
+                wg_ref[side, order] = grads[order][side]
 
     mine = jnp.zeros((half, count), F32)
     theirs = jnp.zeros((half, count), F32)
@@ -245,15 +246,15 @@
 
     if fused:
         total = rs_send[me].astype(F32)
-        for d in range(1, patches):
-            scatter[d - 1].wait_recv()
+        for c, d in zip(scatter, order_of):
+            c.wait_recv()
             total = total + rs_recv[d].astype(F32)
         scale = 1.0 / (count * patches) ** 0.5
         ag_send[...] = (total * scale).astype(BF16)
         low = me < patches // 2
         goal = jnp.where(low, chan, 1 - chan)
         gather = []
-        for d in range(1, patches):
+        for d in order_of:
             to = lax.rem(me + d, patches)
             gather.append(copy(ag_send, ag_recv.at[me], ags.at[d], agr.at[me], (maps, to, goal)))
             gather[-1].start()
@@ -266,6 +267,9 @@
 
     swap.wait_recv()
     out_ref[...] = (mine + pin[...]).astype(BF16)
+    save_out = pltpu.make_async_copy(out_ref, out_hbm, store.at[0])
+    save_out.start()
+    save_wg = pltpu.make_async_copy(wg_ref, wg_hbm, store.at[1])
 
     if fused:
         size = 2 * half // patches
@@ -285,6 +289,7 @@
                 wg_ref[order, j * size : (j + 1) * size, :] = jnp.where(
                     chan == 0, jnp.concatenate([a, b], axis=1), jnp.concatenate([b, a], axis=1)
                 )
+        save_wg.start()
         for c in scatter:
             c.wait_send()
         for c in gather:
@@ -294,6 +299,10 @@
     pl.when(has_prev)(each(to_prev, "wait_send"))
     each(to_partner, "wait_send")()
     swap.wait_send()
+    if not fused:
+        save_wg.start()
+    save_out.wait()
+    save_wg.wait()
 
 
 def on_device(features, out_grad, cheb_weights, band_offsets, edge_weight):
@@ -309,6 +318,9 @@
     else:
         outs.append(jax.ShapeDtypeStruct((2, ORDERS, half, half), F32))
     scratch = [
+        pltpu.VMEM(outs[0].shape, outs[0].dtype),
+        pltpu.VMEM(outs[1].shape, outs[1].dtype),
+        pltpu.SemaphoreType.DMA((2,)),
         pltpu.VMEM((half, count), BF16),
         pltpu.VMEM((ORDERS, half, 2 * half), BF16),
         pltpu.VMEM((SLOTS, count), jnp.int32),
@@ -341,12 +353,12 @@
             pltpu.SemaphoreType.DMA((patches,)),
             pltpu.SemaphoreType.REGULAR((3,)),
         ]
-    vmem = pl.BlockSpec(memory_space=pltpu.VMEM)
+    hbm = pl.BlockSpec(memory_space=pltpu.HBM)
     grad, weight = pl.pallas_call(
         functools.partial(kernel, patches, fused),
         out_shape=outs,
-        in_specs=[pl.BlockSpec(memory_space=pltpu.HBM)] * 5,
-        out_specs=[vmem] * 2,
+        in_specs=[hbm] * 5,
+        out_specs=[hbm] * 2,
         scratch_shapes=scratch,
         compiler_params=pltpu.CompilerParams(
             collective_id=0, has_side_effects=True, vmem_limit_bytes=63 * 1024 * 1024

time: 23 us -> 22.9 us (level)
  no operation moved by 1% of the time
where the time goes in v4:
time: 22.9 us; the launch traced here: 22.7 us
  Pallas kernels  19.8 us (86%)
  local copies, waits for them, and re-layouts  2.21 us (10%)
  between operations  0.65 us (3%)
    pallas_call x1, Pallas kernels, on_device(): pl.pallas_call(functools.partial(kernel, patches, fused), out_shape=outs,...  19.8 us
    unnamed x4, local copies, waits for them, and re-layouts  2.21 us

profile of v4, /device:TPU:0, one launch (start us, length us, event | category | flops | bytes accessed | tf_op | source)
XLA Modules:
  0.0 22.7 jit_solution(1302444372007323074)
XLA Ops:
  0.6 19.8 %shard_map.68 = (bf16[64,768]{1,0:T(8,128)(2,1)}, bf16[5,64,128]{2,1,0:T(8,128)(2,1)}) custom-call(bf16[64,768]{1,0:T(8,128)(2,1)} %bitcast.5, bf16[64,768]{1,0:T(8,128)(2,1)} %bitcast.6, bf16[5,64,128]{2,1,0:T(8,128)(2,1)} %w_hbm.1, s32[8,768]{1,0:T(8,128)} %bitcast.8, bf16[8,768]{1,0:T(8,128)(2,1)} %bitcast.9), custom_call_target="tpu_custom_call" | custom-call | tf_op jit(solution)/shard_map/pallas_call | solution.py:357
  20.5 0.0 copy-start
  20.5 1.6 %copy.9 = bf16[64,1,768]{2,0,1:T(8,128)(2,1)} copy(bf16[64,1,768]{2,0,1:T(8,128)(2,1)} %bitcast.7) | data formatting | bytes 196608
  22.0 0.0 copy-done
  22.0 0.6 %copy.10 = bf16[5,64,128]{2,1,0:T(8,128)(2,1)} copy(bf16[5,64,128]{2,1,0:T(8,128)(2,1)S(1)} %copy-done) | data formatting | bytes 163840
Async XLA Ops:
  20.5 1.6 %copy-start = (bf16[5,64,128]{2,1,0:T(8,128)(2,1)S(1)}, bf16[5,64,128]{2,1,0:T(8,128)(2,1)}, u32[]{:S(2)}) copy-start(bf16[5,64,128]{2,1,0:T(8,128)(2,1)} %get-tuple-element.9) | copy-start | bytes 245764
